TPU v7x, 32 devices: a whole 2x2x4 slice. The times are simulated.
32 devices in a mesh: dom: 16 (over z, y, x), level: 2 (over core).
Axes of the slice: x: 2, y: 2, z: 4, core: 2. Of those that a mesh axis runs over, the one named last changes fastest.
Arguments:
- residual: float32 [1024, 32, 256], P(('dom', 'level')), may hold values from -6 to 6
- neighbours: int32 [1024, 2], P(('dom', 'level')), may hold values from 0 to 1023, as said below
- pattern: int32 [1024, 6], P(('dom', 'level')), may hold values 0 or 1
- diag_inverse: bfloat16 [1024, 4, 4096], P(('dom', 'level')), may hold values from -2.5 to 2.5
- lower_blocks: bfloat16 [1024, 6, 4096], P(('dom', 'level')), may hold values from -0.44921875 to 0.44921875
- phi: bfloat16 [1024, 192, 256], P(('dom', 'level')), may hold values from -0.375 to 0.375
- aggregate: int32 [1024], P(('dom', 'level')), may hold values from 0 to 127, as said below
- level1_restrict: bfloat16 [196608, 192], P(('dom', 'level')), may hold values from -0.4375 to 0.4375
- level2_interior_solve: bfloat16 [24576, 192], P(('dom', 'level')), may hold values from -1 to 1
- level2_restrict: bfloat16 [24576, 192], P(('dom', 'level')), may hold values from -0.4375 to 0.4375
- level3_interior_solve: bfloat16 [3072, 192], P('dom'), may hold values from -1 to 1
- level3_restrict: bfloat16 [3072, 192], P('dom'), may hold values from -0.4375 to 0.4375
- level4_interior_solve: bfloat16 [384, 192], replicated, may hold values from -1 to 1
- level4_restrict: bfloat16 [384, 192], replicated, may hold values from -0.4375 to 0.4375
- top_inverse: bfloat16 [192, 192], replicated, may hold values from -1 to 1
Outputs:
- correction: float32 [1024, 32, 256], P(('dom', 'level'))
Inputs may be any that keep to these rules, and one draw needn't show every extreme that they name: Subdomains come in blocks of 32 consecutive ones. neighbours[s, 0] lies in the block before s's own (in s's own block for the first block) and neighbours[s, 1] in the block after (in s's own block for the last); each column names every subdomain of such a target block exactly once from the block that points at it. Every aggregate holds exactly 8 subdomains of one block of 32 consecutive subdomains; block b holds the aggregates b * 4 to (b + 1) * 4 - 1.
All inputs are finite; a program needn't handle non-finite values. No bound on the sum of `pattern` on one device may be relied on, other than what follows from the above.
Results may differ from a plain program's by a relative error of at most 0.0003.
Values sent between devices are 32-bit elements; how exact they have to be, the bound alone decides.
A program may use at most 128 MiB of HBM per device.

v0:
```python
import jax
import jax.numpy as jnp
from jax import lax
from jax.sharding import PartitionSpec as P

FULL_ACCURACY = lax.Precision.HIGHEST


def padded_2(x, sides, width):
    for axis, dim in sides:
        size, length = (lax.axis_size(axis), x.shape[dim])
        up = [(i, (i + 1) % size) for i in range(size - 1)]
        down = [(j, i) for i, j in up]
        last = lax.slice_in_dim(x, length - width, length, axis=dim)
        leading = lax.slice_in_dim(x, 0, width, axis=dim)
        before = lax.ppermute(last, axis, up)
        after = lax.ppermute(leading, axis, down)
        x = jnp.concatenate([before, x, after], axis=dim)
    return x


def pair_index(upper_block, lower_block):
    return upper_block * (upper_block - 1) // 2 + lower_block


def block_apply(blocks, vector, transpose):
    block_width = vector.shape[2]
    square = blocks.astype(jnp.float32).reshape(blocks.shape[0], block_width, block_width)
    if transpose:
        return jnp.einsum("sio,sri->sro", square, vector, precision=FULL_ACCURACY)
    return jnp.einsum("soi,sri->sro", square, vector, precision=FULL_ACCURACY)


def forward_block(sources, forward, block_id, pair_mask, lower_blocks):
    current = sources[block_id]
    for prior_id in range(block_id):
        pair_slot = pair_index(block_id, prior_id)
        current = current - pair_mask[:, pair_slot][:, None, None] * block_apply(
            lower_blocks[:, pair_slot], forward[prior_id], False
        )
    return current


def finish_solve(forward, pair_mask, diag_inverse, lower_blocks):
    block_count = len(forward)
    middle = [
        block_apply(diag_inverse[:, block_id], forward[block_id], False)
        for block_id in range(block_count)
    ]
    result = [None] * block_count
    for block_id in reversed(range(block_count)):
        current = middle[block_id]
        for later_id in range(block_id + 1, block_count):
            pair_slot = pair_index(later_id, block_id)
            current = current - pair_mask[:, pair_slot][:, None, None] * block_apply(
                lower_blocks[:, pair_slot], result[later_id], True
            )
        result[block_id] = current
    return jnp.concatenate(result, axis=2)


def per_device(
    residual,
    neighbours,
    pattern,
    diag_inverse,
    lower_blocks,
    phi,
    aggregate,
    level1_restrict,
    level2_interior_solve,
    level2_restrict,
    level3_interior_solve,
    level3_restrict,
    level4_interior_solve,
    level4_restrict,
    top_inverse,
):
    sub_dev, rhs_count, sub_dofs = residual.shape
    nblocks = diag_inverse.shape[1]
    block_width = sub_dofs // nblocks
    iface_dofs = 2 * block_width
    coarse_count = top_inverse.shape[0]
    aggregates_device_share = sub_dev // 8
    pair_mask = pattern.astype(jnp.float32)
    sources = [
        residual[:, :, block_id * block_width : (block_id + 1) * block_width]
        for block_id in range(nblocks - 2)
    ]
    forward = []
    for block_id in range(nblocks - 2):
        forward.append(forward_block(sources, forward, block_id, pair_mask, lower_blocks))
    device = lax.axis_index(("dom", "level"))
    edge_rows = residual[:, :, sub_dofs - iface_dofs :]
    padded = padded_2(edge_rows, ((("dom", "level"), 0),), sub_dev)
    base_row = (device - 1) * sub_dev
    from_left = jnp.take(padded, neighbours[:, 0] - base_row, axis=0)
    from_right = jnp.take(padded, neighbours[:, 1] - base_row, axis=0)
    assembled = (edge_rows + from_left + from_right) / 3.0
    assembled_rhs = jnp.concatenate([residual[:, :, : sub_dofs - iface_dofs], assembled], axis=2)
    for block_id in range(nblocks - 2, nblocks):
        sources.append(assembled_rhs[:, :, block_id * block_width : (block_id + 1) * block_width])
    for block_id in range(nblocks - 2, nblocks):
        forward.append(forward_block(sources, forward, block_id, pair_mask, lower_blocks))
    fine_x = finish_solve(forward, pair_mask, diag_inverse, lower_blocks)
    phi_values = phi.astype(jnp.float32)
    level1_mats = level1_restrict.astype(jnp.float32).reshape(sub_dev, coarse_count, coarse_count)
    coarse_rhs = jnp.einsum("ski,sri->srk", phi_values, assembled_rhs, precision=FULL_ACCURACY)
    level1_terms = jnp.einsum("sri,sij->srj", coarse_rhs, level1_mats, precision=FULL_ACCURACY)
    local_owner = aggregate - device * aggregates_device_share
    owner_table = (
        local_owner[:, None] == jnp.arange(aggregates_device_share, dtype=jnp.int32)[None, :]
    ).astype(jnp.float32)
    level2_residual = jnp.einsum("sa,srj->arj", owner_table, level1_terms, precision=FULL_ACCURACY)
    level2_matrices = level2_restrict.astype(jnp.float32).reshape(
        aggregates_device_share, coarse_count, coarse_count
    )
    level2_eliminated = level2_interior_solve.astype(jnp.float32).reshape(
        aggregates_device_share, coarse_count, coarse_count
    )
    level2_terms = jnp.einsum(
        "ari,aij->rj", level2_residual, level2_matrices, precision=FULL_ACCURACY
    )
    level3_residual = lax.psum(level2_terms, "level")
    level3_matrices = level3_restrict.astype(jnp.float32)
    level3_eliminated = level3_interior_solve.astype(jnp.float32)
    level3_terms = jnp.dot(level3_residual, level3_matrices, precision=FULL_ACCURACY)
    dom_index = lax.axis_index("dom")
    group_id = dom_index // 8
    top_values = top_inverse.astype(jnp.float32)
    group_count = lax.axis_size("dom") // 8
    slots = jnp.where(
        (jnp.arange(group_count, dtype=jnp.int32) == group_id)[:, None, None],
        level3_terms[None],
        0.0,
    )
    totals = lax.psum(slots, "dom")
    level4_residual = lax.dynamic_index_in_dim(totals, group_id, 0, keepdims=False)
    restrict_all = level4_restrict.astype(jnp.float32).reshape(
        group_count, coarse_count, coarse_count
    )
    top_resid = jnp.einsum("pri,pij->rj", totals, restrict_all, precision=FULL_ACCURACY)
    top_correction = jnp.dot(top_resid, top_values.T, precision=FULL_ACCURACY)
    own_restrict = lax.dynamic_index_in_dim(restrict_all, group_id, 0, keepdims=False)
    own_interior = lax.dynamic_slice_in_dim(
        level4_interior_solve, group_id * coarse_count, coarse_count, 0
    ).astype(jnp.float32)
    level4_correction = jnp.dot(level4_residual, own_interior.T, precision=FULL_ACCURACY) + jnp.dot(
        top_correction, own_restrict.T, precision=FULL_ACCURACY
    )
    level3_correction = jnp.dot(
        level3_residual, level3_eliminated.T, precision=FULL_ACCURACY
    ) + jnp.dot(level4_correction, level3_matrices.T, precision=FULL_ACCURACY)
    level2_correction = jnp.einsum(
        "bpf,bxf->bxp", level2_eliminated, level2_residual, precision=FULL_ACCURACY
    ) + jnp.einsum("aij,rj->ari", level2_matrices, level3_correction, precision=FULL_ACCURACY)
    owner_corr = jnp.einsum("sa,arj->srj", owner_table, level2_correction, precision=FULL_ACCURACY)
    coarse_corr = jnp.einsum("sij,srj->sri", level1_mats, owner_corr, precision=FULL_ACCURACY)
    return fine_x + jnp.einsum("ski,srk->sri", phi_values, coarse_corr, precision=FULL_ACCURACY)


def solution(mesh):
    in_specs = (
        P(("dom", "level"), None, None),
        P(("dom", "level"), None),
        P(("dom", "level"), None),
        P(("dom", "level"), None, None),
        P(("dom", "level"), None, None),
        P(("dom", "level"), None, None),
        P(("dom", "level")),
        P(("dom", "level"), None),
        P(("dom", "level"), None),
        P(("dom", "level"), None),
        P("dom", None),
        P("dom", None),
        P(),
        P(),
        P(),
    )
    out_specs = P(("dom", "level"), None, None)
    return jax.shard_map(
        per_device, mesh=mesh, in_specs=in_specs, out_specs=out_specs, check_vma=False
    )
```

profile of v0, /device:TPU:0, one launch (start us, length us, event | category | flops | bytes accessed | tf_op | source)
XLA Modules:
  0.0 195.8 jit_solution(13770734075171863457)
XLA Ops:
  0.0 2.0 %slice.91 = f32[32,32,128]{2,1,0:T(8,128)} slice(f32[32,32,256]{2,1,0:T(8,128)} %param.17), slice={[0:32], [0:32], [128:256]} | slice | bytes 1048576 | tf_op jit(solution)/shard_map/slice | solution.py:94
  2.0 1.3 collective-permute-start.1
  3.3 3.8 %collective-permute-start = (f32[32,32,128]{2,1,0:T(8,128)}, f32[32,32,128]{2,1,0:T(8,128)}, u32[]{:S(2)}, u32[]{:S(2)}) collective-permute-start(f32[32,32,128]{2,1,0:T(8,128)} %slice.91), channel_id=1, source_target_pairs={{0,1},{1,2},{2,3},{3,4},{4,5},{5,6},{6,7},{7,8},{8,9},{9,10},{10,1... | collective-permute-start | bytes 1572872 | tf_op jit(solution)/shard_map/ppermute | solution.py:16
  7.6 6.4 %reshape.89 = bf16[32,192,192]{1,0,2:T(8,128)(2,1)} reshape(bf16[6144,192]{0,1:T(8,128)(2,1)} %param.24) | data formatting | bytes 4718592 | tf_op jit(solution)/shard_map/reshape | solution.py:107
  15.2 1.3 reshape.91
  16.5 1.7 copy.20
  18.3 2.6 %fusion.53 = (bf16[32,1,4096]{2,0,1:T(8,128)(2,1)}, bf16[32,1,4096]{2,0,1:T(8,128)(2,1)}, bf16[32,1,4096]{2,0,1:T(8,128)(2,1)}, bf16[32,1,4096]{2,0,1:T(8,128)(2...) fusion(bf16[32,6,4096]{2,0,1:T(8,128)(2,1)} %param.21), kind=kLoop, calls=%fused_computation.94 | loop fusion | bytes 3145728 | tf_op jit(solution)/shard_map/slice | solution.py:39
  20.8 2.3 %reshape.85 = bf16[32,64,64]{2,1,0:T(8,128)(2,1)} reshape(bf16[32,1,4096]{2,0,1:T(8,128)(2,1)} %get-tuple-element.15) | data formatting | bytes 524288 | tf_op jit(solution)/shard_map/reshape | solution.py:28
  23.7 2.3 %reshape.80 = bf16[32,64,64]{2,1,0:T(8,128)(2,1)} reshape(bf16[32,1,4096]{2,0,1:T(8,128)(2,1)} %get-tuple-element.18) | data formatting | bytes 524288 | tf_op jit(solution)/shard_map/reshape | solution.py:28
  25.9 2.3 %reshape.86 = bf16[32,64,64]{2,1,0:T(8,128)(2,1)} reshape(bf16[32,1,4096]{2,0,1:T(8,128)(2,1)} %get-tuple-element.19) | data formatting | bytes 524288 | tf_op jit(solution)/shard_map/reshape | solution.py:28
  28.2 2.3 %reshape.82 = bf16[32,64,64]{2,1,0:T(8,128)(2,1)} reshape(bf16[32,1,4096]{2,0,1:T(8,128)(2,1)} %get-tuple-element.17) | data formatting | bytes 524288 | tf_op jit(solution)/shard_map/reshape | solution.py:28
  30.5 2.3 %reshape.83 = bf16[32,64,64]{2,1,0:T(8,128)(2,1)} reshape(bf16[32,1,4096]{2,0,1:T(8,128)(2,1)} %get-tuple-element.16) | data formatting | bytes 524288 | tf_op jit(solution)/shard_map/reshape | solution.py:28
  32.8 2.3 %reshape.87 = bf16[32,64,64]{2,1,0:T(8,128)(2,1)} reshape(bf16[32,1,4096]{2,0,1:T(8,128)(2,1)} %get-tuple-element.14) | data formatting | bytes 524288 | tf_op jit(solution)/shard_map/reshape | solution.py:28
  35.0 8.5 %slice_reduce_fusion.3 = (bf16[32,4096]{1,0:T(8,128)(2,1)}, bf16[32,4096]{1,0:T(8,128)(2,1)}, bf16[32,4096]{1,0:T(8,128)(2,1)}, bf16[32,4096]{1,0:T(8,128)(2,1)}) fusion(bf16[32,4,4096]{2,1,0:T(4,128)(2,1)} %param.20), kind=kLoop, calls=%fused_computation.52 | loop fusion | bytes 2097152 | tf_op jit(solution)/shard_map/slice | solution.py:47
  43.5 2.3 %reshape.88 = bf16[32,64,64]{2,1,0:T(8,128)(2,1)} reshape(bf16[32,4096]{1,0:T(8,128)(2,1)} %get-tuple-element.8) | data formatting | bytes 524288 | tf_op jit(solution)/shard_map/reshape | solution.py:28
  45.8 2.3 %reshape.84 = bf16[32,64,64]{2,1,0:T(8,128)(2,1)} reshape(bf16[32,4096]{1,0:T(8,128)(2,1)} %get-tuple-element.9) | data formatting | bytes 524288 | tf_op jit(solution)/shard_map/reshape | solution.py:28
  48.1 2.3 %reshape.81 = bf16[32,64,64]{2,1,0:T(8,128)(2,1)} reshape(bf16[32,4096]{1,0:T(8,128)(2,1)} %get-tuple-element.7) | data formatting | bytes 524288 | tf_op jit(solution)/shard_map/reshape | solution.py:28
  50.4 2.3 %reshape.79 = bf16[32,64,64]{2,1,0:T(8,128)(2,1)} reshape(bf16[32,4096]{1,0:T(8,128)(2,1)} %get-tuple-element.6) | data formatting | bytes 524288 | tf_op jit(solution)/shard_map/reshape | solution.py:28
  54.4 2.3 %fusion.15 = f32[32,32,64]{2,1,0:T(8,128)S(1)} fusion(bf16[32,64,64]{2,1,0:T(8,128)(2,1)} %reshape.80, f32[32,32,256]{2,1,0:T(8,128)} %param.17, f32[32]{0:T(128)} %get-tuple-element.27), kind=kOutput, calls=%fused_computation.31 | convolution fusion | flops 50462720 | bytes 1572992 | tf_op jit(solution)/shard_map/soi,sri->sro/dot_general | solution.py:31
  56.8 3.1 %fusion.29 = f32[32,32,64]{2,1,0:T(8,128)} fusion(bf16[32,64,64]{2,1,0:T(8,128)(2,1)} %reshape.79, f32[32,32,256]{2,1,0:T(8,128)} %param.17), kind=kOutput, calls=%fused_computation.56 | convolution fusion | flops 50331648 | bytes 1310720 | tf_op jit(solution)/shard_map/soi,sri->sro/dot_general | solution.py:31
  60.0 1.7 fusion.55
  61.7 2.6 %pad_maximum_fusion = f32[96,32,128]{2,1,0:T(8,128)} fusion(f32[32,32,128]{2,1,0:T(8,128)} %collective-permute-done.1, f32[32,32,128]{2,1,0:T(8,128)} %slice.91, f32[32,32,128]{2,1,0:T(8,128)} %collective-permute-done), kind=kLoop, calls=%fused_computation.6 | loop fusion | flops 786432 | bytes 3145728 | tf_op jit(solution)/shard_map/concatenate | solution.py:18
  64.3 2.8 %gather_fusion.1 = f32[32,32,128]{2,1,0:T(8,128)} fusion(f32[96,32,128]{2,1,0:T(8,128)} %pad_maximum_fusion, s32[1024]{0:T(1024)S(1)} %get-tuple-element.30), kind=kCustom, calls=%fused_computation.1.clone | custom fusion | bytes 1048704 | tf_op jit(solution)/shard_map/jit(_take)/gather | solution.py:98
  67.1 2.8 %gather_fusion = f32[32,32,128]{2,1,0:T(8,128)} fusion(f32[96,32,128]{2,1,0:T(8,128)} %pad_maximum_fusion, s32[1024]{0:T(1024)S(1)} %get-tuple-element.31), kind=kCustom, calls=%fused_computation.clone | custom fusion | bytes 1048704 | tf_op jit(solution)/shard_map/jit(_take)/gather | solution.py:97
  69.9 1.7 fusion.54
  71.7 2.9 %fusion.18 = f32[32,32,192]{2,1,0:T(8,128)S(1)} fusion(bf16[32,192,256]{2,1,0:T(8,128)(2,1)S(1)} %copy-done, f32[32,32,128]{2,1,0:T(8,128)S(1)} %get-tuple-element.21, f32[32,32,128]{2,1,0:T(8,128)S(1)} %get-tuple-element.20), kind=kOutput, calls=%fused_computation.39 | convolution fusion | flops 604241920 | bytes 4980736 | tf_op jit(solution)/shard_map/ski,sri->srk/dot_general | solution.py:108
  74.7 3.9 %fusion = f32[32,32,192]{2,1,0:T(8,128)S(1)} fusion(f32[32,32,192]{2,1,0:T(8,128)S(1)} %fusion.18, bf16[32,192,192]{1,0,2:T(8,128)(2,1)S(1)} %copy-done.1), kind=kOutput, calls=%fused_computation.2 | convolution fusion | flops 452984832 | bytes 3932160 | tf_op jit(solution)/shard_map/sri,sij->srj/dot_general | solution.py:109
  81.7 6.2 %psum.14 = f32[32,192]{1,0:T(8,128)} all-reduce(f32[32,192]{1,0:T(8,128)} %convolution_bitcast_fusion.2), channel_id=1, replica_groups=mesh['dom'=16,'level'=2] {'level'}, use_global_device_ids=true, to_apply=%region_0.0 | all-reduce | flops 6144 | bytes 49152 | tf_op jit(solution)/shard_map/psum | solution.py:124
  88.0 1.8 fusion.58
  91.5 78.3 %psum.15 = f32[2,32,192]{2,1,0:T(8,128)} all-reduce(f32[2,32,192]{2,1,0:T(8,128)} %broadcast_select_fusion), channel_id=1, replica_groups=mesh['dom'=16,'level'=2] {'dom'}, use_global_device_ids=true, to_apply=%region_1.3 | all-reduce | flops 12288 | bytes 98304 | tf_op jit(solution)/shard_map/psum | solution.py:137
  177.5 5.4 %fusion.2 = f32[32,32,192]{2,1,0:T(8,128)S(1)} fusion(bf16[32,192,192]{1,0,2:T(8,128)(2,1)} %reshape.89, f32[32,32,192]{2,0,1:T(8,128)S(1)} %fusion.35), kind=kOutput, calls=%fused_computation.4 | convolution fusion | flops 452984832 | bytes 3932160 | tf_op jit(solution)/shard_map/sij,srj->sri/dot_general | solution.py:158
  193.0 2.8 %convolution_add_fusion = f32[32,32,256]{2,1,0:T(8,128)} fusion(f32[32,32,192]{2,1,0:T(8,128)S(1)} %fusion.2, bf16[32,192,256]{2,1,0:T(8,128)(2,1)S(1)} %copy-done, f32[32,32,64]{2,1,0:T(8,128)S(1)} %fusion.57, f32[32,32,64]{2,1,0:T(8,128)S(1)} %fusion.9, f32[32,32,64]{2,1,0:T(8,128)S(1)} %fusion.7, f32[32,32,64]{2,1,0:T(8,128)S(1)} %fusion.4), kind=kOutput, calls=%fused_computation.7 | convolution fusion | flops 605028352 | bytes 6029312 | tf_op jit(solution)/shard_map/ski,srk->sri/dot_general | solution.py:159
  (90 shorter events, 26.3 us)
Async XLA Ops:
  0.0 71.7 %copy-start = (bf16[32,192,256]{2,1,0:T(8,128)(2,1)S(1)}, bf16[32,192,256]{2,1,0:T(8,128)(2,1)}, u32[]{:S(2)}) copy-start(bf16[32,192,256]{2,1,0:T(8,128)(2,1)} %param.22) | copy-start | bytes 9437188
  0.0 14.1 %copy-start.19 = (bf16[768,192]{0,1:T(8,128)(2,1)S(1)}, bf16[768,192]{0,1:T(8,128)(2,1)}, u32[]{:S(2)}) copy-start(bf16[768,192]{0,1:T(8,128)(2,1)} %param.25) | copy-start | bytes 884740
  2.0 59.7 %collective-permute-start.1 = (f32[32,32,128]{2,1,0:T(8,128)}, f32[32,32,128]{2,1,0:T(8,128)}, u32[]{:S(2)}, u32[]{:S(2)}) collective-permute-start(f32[32,32,128]{2,1,0:T(8,128)} %slice.91), channel_id=1, source_target_pairs={{1,0},{2,1},{3,2},{4,3},{5,4},{6,5},{7,6},{8,7},{9,8},{10,9},{11,1... | collective-permute-start | bytes 1572872 | tf_op jit(solution)/shard_map/ppermute | solution.py:17
  3.3 58.4 %collective-permute-start = (f32[32,32,128]{2,1,0:T(8,128)}, f32[32,32,128]{2,1,0:T(8,128)}, u32[]{:S(2)}, u32[]{:S(2)}) collective-permute-start(f32[32,32,128]{2,1,0:T(8,128)} %slice.91), channel_id=1, source_target_pairs={{0,1},{1,2},{2,3},{3,4},{4,5},{5,6},{6,7},{7,8},{8,9},{9,10},{10,1... | collective-permute-start | bytes 1572872 | tf_op jit(solution)/shard_map/ppermute | solution.py:16
  14.1 9.0 %copy-start.24 = (s32[32,6]{0,1:T(8,128)S(1)}, s32[32,6]{0,1:T(8,128)}, u32[]{:S(2)}) copy-start(s32[32,6]{0,1:T(8,128)} %param.19) | copy-start | bytes 2308
  35.0 17.6 %copy-start.26 = (s32[32,2]{0,1:T(2,128)S(1)}, s32[32,2]{0,1:T(2,128)}, u32[]{:S(2)}) copy-start(s32[32,2]{0,1:T(2,128)} %param.18) | copy-start | bytes 772
  54.4 5.5 %copy-start.17 = (bf16[32,64,64]{2,1,0:T(8,128)(2,1)S(1)}, bf16[32,64,64]{2,1,0:T(8,128)(2,1)}, u32[]{:S(2)}) copy-start(bf16[32,64,64]{2,1,0:T(8,128)(2,1)} %reshape.81) | copy-start | bytes 786436
  56.8 3.1 %copy-start.3 = (f32[32,32,64]{2,1,0:T(8,128)}, f32[32,32,64]{2,1,0:T(8,128)S(1)}, u32[]{:S(2)}) copy-start(f32[32,32,64]{2,1,0:T(8,128)S(1)} %fusion.15) | copy-start | bytes 786436
  71.7 7.0 %copy-start.5 = (f32[32,32,128]{2,1,0:T(8,128)}, f32[32,32,128]{2,1,0:T(8,128)S(1)}, u32[]{:S(2)}) copy-start(f32[32,32,128]{2,1,0:T(8,128)S(1)} %get-tuple-element.21) | copy-start | bytes 1572868
  71.7 3.0 %copy-start.1 = (bf16[32,192,192]{1,0,2:T(8,128)(2,1)S(1)}, bf16[32,192,192]{1,0,2:T(8,128)(2,1)}, u32[]{:S(2)}) copy-start(bf16[32,192,192]{1,0,2:T(8,128)(2,1)} %reshape.89) | copy-start | bytes 7077892
  74.7 4.0 %copy-start.25 = (s32[32]{0:T(128)S(1)}, s32[32]{0:T(128)}, u32[]{:S(2)}) copy-start(s32[32]{0:T(128)} %broadcast_subtract_fusion) | copy-start | bytes 388
  74.7 5.0 %copy-start.18 = (bf16[4,192,192]{1,0,2:T(4,128)(2,1)S(1)}, bf16[4,192,192]{1,0,2:T(4,128)(2,1)}, u32[]{:S(2)}) copy-start(bf16[4,192,192]{1,0,2:T(4,128)(2,1)} %reshape.90) | copy-start | bytes 884740
  74.7 16.2 %copy-start.27 = (pred[2]{0:T(512)(128)(4,1)S(1)}, pred[2]{0:T(512)(128)(4,1)}, u32[]{:S(2)}) copy-start(pred[2]{0:T(512)(128)(4,1)} %iota_compare_fusion.1) | copy-start | bytes 10
  176.9 6.1 %copy-start.2 = (f32[32,32,256]{2,1,0:T(8,128)S(1)}, f32[32,32,256]{2,1,0:T(8,128)}, u32[]{:S(2)}) copy-start(f32[32,32,256]{2,1,0:T(8,128)} %param.17) | copy-start | bytes 3145732
  176.9 6.1 %copy-start.6 = (f32[32,32,128]{2,1,0:T(8,128)S(1)}, f32[32,32,128]{2,1,0:T(8,128)}, u32[]{:S(2)}) copy-start(f32[32,32,128]{2,1,0:T(8,128)} %copy-done.5) | copy-start | bytes 1572868
  176.9 6.1 %copy-start.7 = (bf16[32,64,64]{2,1,0:T(8,128)(2,1)S(1)}, bf16[32,64,64]{2,1,0:T(8,128)(2,1)}, u32[]{:S(2)}) copy-start(bf16[32,64,64]{2,1,0:T(8,128)(2,1)} %reshape.85) | copy-start | bytes 786436
  177.5 6.4 %copy-start.8 = (bf16[32,64,64]{2,1,0:T(8,128)(2,1)S(1)}, bf16[32,64,64]{2,1,0:T(8,128)(2,1)}, u32[]{:S(2)}) copy-start(bf16[32,64,64]{2,1,0:T(8,128)(2,1)} %reshape.82) | copy-start | bytes 786436
  182.9 2.0 %copy-start.4 = (f32[32,32,64]{2,1,0:T(8,128)S(1)}, f32[32,32,64]{2,1,0:T(8,128)}, u32[]{:S(2)}) copy-start(f32[32,32,64]{2,1,0:T(8,128)} %copy-done.3) | copy-start | bytes 786436
  183.0 2.0 %copy-start.10 = (bf16[32,64,64]{2,1,0:T(8,128)(2,1)S(1)}, bf16[32,64,64]{2,1,0:T(8,128)(2,1)}, u32[]{:S(2)}) copy-start(bf16[32,64,64]{2,1,0:T(8,128)(2,1)} %reshape.83) | copy-start | bytes 786436
  183.0 2.0 %copy-start.22 = (f32[32]{0:T(128)S(1)}, f32[32]{0:T(128)}, u32[]{:S(2)}) copy-start(f32[32]{0:T(128)} %get-tuple-element.26) | copy-start | bytes 388
  183.0 2.9 %copy-start.16 = (bf16[32,64,64]{2,1,0:T(8,128)(2,1)S(1)}, bf16[32,64,64]{2,1,0:T(8,128)(2,1)}, u32[]{:S(2)}) copy-start(bf16[32,64,64]{2,1,0:T(8,128)(2,1)} %reshape.84) | copy-start | bytes 786436
  184.0 2.9 %copy-start.9 = (bf16[32,64,64]{2,1,0:T(8,128)(2,1)S(1)}, bf16[32,64,64]{2,1,0:T(8,128)(2,1)}, u32[]{:S(2)}) copy-start(bf16[32,64,64]{2,1,0:T(8,128)(2,1)} %reshape.86) | copy-start | bytes 786436
  184.0 2.9 %copy-start.21 = (f32[32]{0:T(128)S(1)}, f32[32]{0:T(128)}, u32[]{:S(2)}) copy-start(f32[32]{0:T(128)} %get-tuple-element.23) | copy-start | bytes 388
  184.9 2.9 %copy-start.11 = (bf16[32,64,64]{2,1,0:T(8,128)(2,1)S(1)}, bf16[32,64,64]{2,1,0:T(8,128)(2,1)}, u32[]{:S(2)}) copy-start(bf16[32,64,64]{2,1,0:T(8,128)(2,1)} %reshape.87) | copy-start | bytes 786436
  184.9 2.9 %copy-start.23 = (f32[32]{0:T(128)S(1)}, f32[32]{0:T(128)}, u32[]{:S(2)}) copy-start(f32[32]{0:T(128)} %get-tuple-element.22) | copy-start | bytes 388
  185.9 2.9 %copy-start.15 = (bf16[32,64,64]{2,1,0:T(8,128)(2,1)S(1)}, bf16[32,64,64]{2,1,0:T(8,128)(2,1)}, u32[]{:S(2)}) copy-start(bf16[32,64,64]{2,1,0:T(8,128)(2,1)} %reshape.88) | copy-start | bytes 786436
  187.8 2.5 %copy-start.14 = (f32[32,32,64]{2,1,0:T(8,128)S(1)}, f32[32,32,64]{2,1,0:T(8,128)}, u32[]{:S(2)}) copy-start(f32[32,32,64]{2,1,0:T(8,128)} %fusion.55) | copy-start | bytes 786436
  189.7 1.7 copy-start.12
  189.7 1.7 copy-start.13
  189.7 1.7 copy-start.20
where the time goes:
time: 197 us; the launch traced here: 196 us
  blocking collectives  84.5 us (43%)
  local copies, waits for them, and re-layouts  52.7 us (27%)
  matrix products  45.6 us (23%)
  other arithmetic  7.32 us (4%)
  starting transfers between devices  5.13 us (3%)
    psum x1, blocking collectives, per_device(): totals = lax.psum(slots, 'dom')  78.3 us
    reshape x10, local copies, waits for them, and re-layouts, block_apply(): blocks.astype(jnp.float32)  22.8 us
    dot_general x10, matrix products, block_apply(): return jnp.einsum('soi,sri->sro', square, vector, precision=FULL_ACCURACY)  13.7 us
    slice x1, local copies, waits for them, and re-layouts, finish_solve(): diag_inverse[:, block_id]  8.49 us
    reshape x1, local copies, waits for them, and re-layouts, per_device(): level1_restrict.astype(jnp.float32)  6.44 us
    psum x1, blocking collectives, per_device(): level3_residual = lax.psum(level2_terms, 'level')  6.24 us
    dot_general x1, matrix products, per_device(): jnp.einsum('sij,srj->sri', level1_mats, owner_corr, precision=FULL_ACCURACY)  5.39 us
  transfers between devices with their start and end apart: 2, of which 0 were waited for; matrix products, arithmetic and copies ran while one was open for 28% of the time, Pallas kernels for 0%

commit v1 on v0

v1 whole, which is shorter than its diff:
```python
import functools

import jax
import jax.numpy as jnp
from jax import lax
from jax.experimental import pallas as pl
from jax.experimental.pallas import tpu as pltpu
from jax.sharding import PartitionSpec as P

MESH = pl.DeviceIdType.MESH
F32 = jnp.float32
BF16 = jnp.bfloat16
GROUP = 8
UNROLL = 4


def split(x):
    hi = x.astype(BF16)
    lo = (x - hi.astype(F32)).astype(BF16)
    return jnp.concatenate([hi, lo], axis=0)


def fold(y):
    half = y.shape[0] // 2
    return y[:half] + y[half:]


def mul(x, w):
    return fold(lax.dot_general(split(x), w, (((1,), (0,)), ((), ())), preferred_element_type=F32))


def mul_t(x, w):
    return fold(lax.dot_general(split(x), w, (((1,), (1,)), ((), ())), preferred_element_type=F32))


def near(ref, i):
    return ref[jnp.clip(i, 0, ref.shape[0] - 1)]


def kernel(
    n_dom,
    n_lev,
    neigh,
    pattern,
    agg,
    res_h,
    diag_h,
    lower_h,
    phi_h,
    l1_h,
    l2i_h,
    l2r_h,
    l3i_h,
    l3r_h,
    l4i_h,
    l4r_h,
    top_h,
    out_h,
    res,
    diag,
    lower,
    phi,
    l1,
    l2i,
    l2r,
    l3i,
    l3r,
    l4i,
    l4r,
    top,
    recv_l,
    recv_r,
    spread,
    wide,
    lmat,
    dmat,
    fine,
    l2res,
    l2corr,
    xsend,
    xrecv,
    totals,
    in_sem,
    halo_send,
    halo_recv,
    own_sem,
    x_send_sem,
    x_recv_sem,
    t_send_sem,
    t_recv_sem,
    out_sem,
):
    subs, rhs, dofs = res.shape
    npair = lower.shape[1]
    nblk = diag.shape[1]
    bs = dofs // nblk
    edge = 2 * bs
    inner = dofs - edge
    width = top.shape[0]
    n_agg = subs // 8
    n_groups = n_dom // GROUP
    tiles = lower.shape[2] // 128
    steps = subs // UNROLL

    dom = lax.axis_index("dom")
    lev = lax.axis_index("level")
    me = dom * n_lev + lev
    last = n_dom * n_lev - 1

    loads = []
    for i, (src, dst) in enumerate(
        [
            (lower_h, lower),
            (diag_h, diag),
            (res_h, res),
            (phi_h, phi),
            (l1_h, l1),
            (l2r_h, l2r),
            (l2i_h, l2i),
            (l3r_h, l3r),
            (l3i_h, l3i),
            (l4r_h, l4r),
            (l4i_h, l4i),
            (top_h, top),
        ]
    ):
        copy = pltpu.make_async_copy(src, dst, in_sem.at[i])
        copy.start()
        loads.append(copy)

    def at(d):
        return (d // n_lev, d % n_lev)

    partners = [(dom, lev + 1 - 2 * (lev % 2))]
    w = 1
    while w < GROUP:
        partners.append((dom + w - 2 * w * ((dom // w) % 2), lev))
        w *= 2
    others = [((dom + GROUP * k) % n_dom, lev) for k in range(1, n_groups)]
    back = [((dom + n_dom - GROUP * k) % n_dom, lev) for k in range(1, n_groups)]
    right = at(jnp.minimum(me + 1, last))
    left = at(jnp.maximum(me - 1, 0))

    barrier = pltpu.get_barrier_semaphore()
    for p in partners + others + back:
        pl.semaphore_signal(barrier, inc=1, device_id=p, device_id_type=MESH)

    @pl.when(me > 0)
    def _():
        pl.semaphore_signal(barrier, inc=1, device_id=left, device_id_type=MESH)

    @pl.when(me < last)
    def _():
        pl.semaphore_signal(barrier, inc=1, device_id=right, device_id_type=MESH)

    count = len(partners) + len(others) + len(back)

    @pl.when((me > 0) & (me < last))
    def _():
        pl.semaphore_wait(barrier, count + 2)

    @pl.when((me == 0) | (me == last))
    def _():
        pl.semaphore_wait(barrier, count + 1)

    edge_src = res_h.at[:, :, pl.ds(inner, edge)]
    to_right = pltpu.make_async_remote_copy(
        src_ref=edge_src,
        dst_ref=recv_l,
        send_sem=halo_send.at[0],
        recv_sem=halo_recv.at[0],
        device_id=right,
        device_id_type=MESH,
    )
    to_left = pltpu.make_async_remote_copy(
        src_ref=edge_src,
        dst_ref=recv_r,
        send_sem=halo_send.at[1],
        recv_sem=halo_recv.at[1],
        device_id=left,
        device_id_type=MESH,
    )
    own_l = pltpu.make_async_copy(edge_src, recv_l, own_sem.at[0])
    own_r = pltpu.make_async_copy(edge_src, recv_r, own_sem.at[1])

    @pl.when(me < last)
    def _():
        to_right.start()

    @pl.when(me == last)
    def _():
        own_r.start()

    @pl.when(me > 0)
    def _():
        to_left.start()

    @pl.when(me == 0)
    def _():
        own_l.start()

    loads[0].wait()
    loads[1].wait()
    wide[...] = jnp.zeros_like(wide)
    l2res[...] = jnp.zeros_like(l2res)
    low_lane = lax.broadcasted_iota(jnp.int32, (tiles, 128), 1) < bs

    def pair_rows(a, b):
        zero = jnp.zeros((tiles, 128), F32)
        a_even = zero if a is None else a
        b_even = zero if b is None else pltpu.roll(b, bs, 1)
        a_odd = zero if a is None else pltpu.roll(a, bs, 1)
        b_odd = zero if b is None else b
        return jnp.where(low_lane, a_even, b_even), jnp.where(low_lane, a_odd, b_odd)

    def unpack(s, carry):
        x = lower[s].astype(F32)
        y = diag[s].astype(F32)
        for t in range(tiles):
            spread[0, pl.ds(t * 8, npair), :] = x[:, t * 128 : (t + 1) * 128]
            spread[1, pl.ds(t * 8, nblk), :] = y[:, t * 128 : (t + 1) * 128]

        def block(kind, i):
            return spread[kind, pl.ds(i, tiles, stride=8), :]

        for b in range(nblk):
            for jp in range(nblk // 2):
                if 2 * jp < b:
                    parts = []
                    for j in (2 * jp, 2 * jp + 1):
                        if j < b:
                            slot = b * (b - 1) // 2 + j
                            parts.append(block(0, slot) * pattern[s, slot].astype(F32))
                        else:
                            parts.append(None)
                    even, odd = pair_rows(*parts)
                    wide[jp, pl.ds(b * bs, tiles, stride=2), :] = even
                    wide[jp, pl.ds(b * bs + 1, tiles, stride=2), :] = odd
            own = block(1, b)
            even, odd = pair_rows(*((own, None) if b % 2 == 0 else (None, own)))
            wide[nblk // 2, pl.ds(b * bs, tiles, stride=2), :] = even
            wide[nblk // 2, pl.ds(b * bs + 1, tiles, stride=2), :] = odd
        for jp in range(nblk // 2):
            lmat[s, :, pl.ds(jp * 128, 128)] = wide[jp].astype(BF16)
        dmat[s] = wide[nblk // 2].astype(BF16)
        return carry

    lax.fori_loop(0, subs, unpack, 0)

    for copy in loads[2:5]:
        copy.wait()

    @pl.when(me < last)
    def _():
        to_right.wait_send()
        to_left.wait_recv()

    @pl.when(me == last)
    def _():
        own_r.wait()

    @pl.when(me > 0)
    def _():
        to_left.wait_send()
        to_right.wait_recv()

    @pl.when(me == 0)
    def _():
        own_l.wait()

    base_l = jnp.maximum(me - 1, 0) * subs
    base_r = jnp.minimum(me + 1, last) * subs
    agg_base = me * n_agg

    def up(g, carry):
        ids = [g * UNROLL + u for u in range(UNROLL)]
        full = []
        for s in ids:
            mine = res[s]
            total = mine[:, inner:] + near(recv_l, neigh[s, 0] - base_l) + near(recv_r, neigh[s, 1] - base_r)
            full.append(jnp.concatenate([mine[:, :inner], total / 3.0], axis=1))
        for s, x in zip(ids, full):
            res[s] = x
        coarse = [mul_t(x, phi[s]) for s, x in zip(ids, full)]
        terms = [
            mul(x, l1[pl.ds(pl.multiple_of(s * width, width), width), :])
            for s, x in zip(ids, coarse)
        ]
        for a in range(n_agg):
            acc = l2res[a]
            for s, x in zip(ids, terms):
                acc = acc + jnp.where(agg[s] - agg_base == a, 1.0, 0.0).astype(F32) * x
            l2res[a] = acc
        return carry

    lax.fori_loop(0, steps, up, 0)

    for copy in loads[5:]:
        copy.wait()

    def fine_step(g, carry):
        ids = [g * UNROLL + u for u in range(UNROLL)]
        base = [res[s] for s in ids]
        x = base
        for _ in range(nblk - 1):
            x = [b - mul_t(v, lmat[s]) for s, b, v in zip(ids, base, x)]
        mid = []
        for s, v in zip(ids, x):
            cols = [
                mul_t(v[:, jp * 128 : (jp + 1) * 128], dmat[s, pl.ds(jp * 128, 128), :])
                for jp in range(nblk // 2)
            ]
            mid.append(jnp.concatenate(cols, axis=1))
        x = mid
        for _ in range(nblk - 1):
            x = [b - mul(v, lmat[s]) for s, b, v in zip(ids, mid, x)]
        for s, v in zip(ids, x):
            fine[s] = v
        return carry

    def exchange(i, value):
        xsend[i] = value
        copy = pltpu.make_async_remote_copy(
            src_ref=xsend.at[i],
            dst_ref=xrecv.at[i],
            send_sem=x_send_sem.at[i],
            recv_sem=x_recv_sem.at[i],
            device_id=partners[i],
            device_id_type=MESH,
        )
        copy.start()
        return copy

    n_gap = len(partners) + 1
    cuts = [steps * i // n_gap for i in range(n_gap + 1)]

    def work(i):
        lax.fori_loop(cuts[i], cuts[i + 1], fine_step, 0)

    part = mul(l2res[0], l2r[pl.ds(0, width), :])
    for a in range(1, n_agg):
        part = part + mul(l2res[a], l2r[pl.ds(a * width, width), :])
    copy = exchange(0, part)
    work(0)
    copy.wait()
    l3res = xsend[0] + xrecv[0]
    value = mul(l3res, l3r[...])
    for i in range(1, len(partners)):
        copy = exchange(i, value)
        work(i)
        copy.wait()
        value = xsend[i] + xrecv[i]
    group = dom // GROUP
    totals[group] = value
    sends = []
    for k in range(1, n_groups):
        copy = pltpu.make_async_remote_copy(
            src_ref=totals.at[group],
            dst_ref=totals.at[group],
            send_sem=t_send_sem.at[k - 1],
            recv_sem=t_recv_sem.at[k - 1],
            device_id=others[k - 1],
            device_id_type=MESH,
        )
        copy.start()
        sends.append(copy)
    work(n_gap - 1)
    for copy in sends:
        copy.wait()

    top_res = mul(totals[0], l4r[pl.ds(0, width), :])
    for p in range(1, n_groups):
        top_res = top_res + mul(totals[p], l4r[pl.ds(p * width, width), :])
    top_corr = mul_t(top_res, top[...])
    at_group = pl.ds(pl.multiple_of(group * width, width), width)
    l4corr = mul_t(totals[group], l4i[at_group, :]) + mul_t(top_corr, l4r[at_group, :])
    l3corr = mul_t(xsend[0] + xrecv[0], l3i[...]) + mul_t(l4corr, l3r[...])
    for a in range(n_agg):
        rows = pl.ds(a * width, width)
        l2corr[a] = mul_t(l2res[a], l2i[rows, :]) + mul_t(l3corr, l2r[rows, :])

    def down(g, carry):
        ids = [g * UNROLL + u for u in range(UNROLL)]
        q = [near(l2corr, agg[s] - agg_base) for s in ids]
        coarse = [
            mul_t(x, l1[pl.ds(pl.multiple_of(s * width, width), width), :]) for s, x in zip(ids, q)
        ]
        both = [mul(x, phi[s]) for s, x in zip(ids, coarse)]
        for s, x in zip(ids, both):
            fine[s] = fine[s] + x
        rows = pl.ds(g * UNROLL, UNROLL)
        pltpu.make_async_copy(fine.at[rows], out_h.at[rows], out_sem.at[g]).start()
        return carry

    lax.fori_loop(0, steps, down, 0)

    def drain(g, carry):
        rows = pl.ds(g * UNROLL, UNROLL)
        pltpu.make_async_copy(fine.at[rows], out_h.at[rows], out_sem.at[g]).wait()
        return carry

    lax.fori_loop(0, steps, drain, 0)


def solution(mesh):
    n_dom, n_lev = mesh.shape["dom"], mesh.shape["level"]

    def per_device(
        residual,
        neighbours,
        pattern,
        diag_inverse,
        lower_blocks,
        phi,
        aggregate,
        level1_restrict,
        level2_interior_solve,
        level2_restrict,
        level3_interior_solve,
        level3_restrict,
        level4_interior_solve,
        level4_restrict,
        top_inverse,
    ):
        subs, rhs, dofs = residual.shape
        width = top_inverse.shape[0]
        nblk = diag_inverse.shape[1]
        edge = 2 * (dofs // nblk)
        tiles = lower_blocks.shape[2] // 128
        n_agg = subs // 8
        n_groups = n_dom // GROUP
        n_x = 4
        large = [
            residual,
            diag_inverse,
            lower_blocks,
            phi,
            level1_restrict,
            level2_interior_solve,
            level2_restrict,
            level3_interior_solve,
            level3_restrict,
            level4_interior_solve,
            level4_restrict,
            top_inverse,
        ]
        scratch = [pltpu.VMEM(a.shape, a.dtype) for a in large]
        scratch += [
            pltpu.VMEM((subs, rhs, edge), F32),
            pltpu.VMEM((subs, rhs, edge), F32),
            pltpu.VMEM((2, tiles * 8, 128), F32),
            pltpu.VMEM((nblk // 2 + 1, dofs, 128), F32),
            pltpu.VMEM((subs, dofs, dofs), BF16),
            pltpu.VMEM((subs, dofs, 128), BF16),
            pltpu.VMEM((subs, rhs, dofs), F32),
            pltpu.VMEM((n_agg, rhs, width), F32),
            pltpu.VMEM((n_agg, rhs, width), F32),
            pltpu.VMEM((n_x, rhs, width), F32),
            pltpu.VMEM((n_x, rhs, width), F32),
            pltpu.VMEM((n_groups, rhs, width), F32),
            pltpu.SemaphoreType.DMA((len(large),)),
            pltpu.SemaphoreType.DMA((2,)),
            pltpu.SemaphoreType.DMA((2,)),
            pltpu.SemaphoreType.DMA((2,)),
            pltpu.SemaphoreType.DMA((n_x,)),
            pltpu.SemaphoreType.DMA((n_x,)),
            pltpu.SemaphoreType.DMA((max(n_groups - 1, 1),)),
            pltpu.SemaphoreType.DMA((max(n_groups - 1, 1),)),
            pltpu.SemaphoreType.DMA((subs // UNROLL,)),
        ]
        return pl.pallas_call(
            functools.partial(kernel, n_dom, n_lev),
            out_shape=jax.ShapeDtypeStruct(residual.shape, F32),
            in_specs=[pl.BlockSpec(memory_space=pltpu.SMEM)] * 3
            + [pl.BlockSpec(memory_space=pl.ANY)] * len(large),
            out_specs=pl.BlockSpec(memory_space=pl.ANY),
            scratch_shapes=scratch,
            compiler_params=pltpu.CompilerParams(
                collective_id=0, has_side_effects=True, vmem_limit_bytes=56 * 2**20
            ),
            cost_estimate=pl.CostEstimate(
                flops=10**9, bytes_accessed=13 * 10**6, transcendentals=0
            ),
        )(neighbours, pattern, aggregate, *large)

    both = P(("dom", "level"))
    in_specs = (both,) * 10 + (P("dom"),) * 2 + (P(),) * 3
    return jax.shard_map(
        per_device, mesh=mesh, in_specs=in_specs, out_specs=both, check_vma=False
    )
```

time: 197 us -> 60.6 us (0.31)
  blocking collectives: 84.5 us -> 0 us
  matrix products: 45.6 us -> 0 us
  Pallas kernels: 0 us -> 41.4 us
  local copies, waits for them, and re-layouts: 52.7 us -> 18.8 us
  other arithmetic: 7.32 us -> 0 us
  starting transfers between devices: 5.13 us -> 0 us
    psum x2 -> x0, blocking collectives: 84.5 us -> none  [the longest x1 78.3 us: per_device(): totals = lax.psum(slots, 'dom')]
    dot_general x32 -> x0, matrix products: 45.6 us -> none  [the longest x10 13.7 us: block_apply(): return jnp.einsum('soi,sri->sro', square, vector, precision=FULL_ACCURACY)]
    pallas_call x0 -> x1, Pallas kernels: none -> 41.4 us  [per_device(): pl.pallas_call(functools.partial(kernel, n_dom, n_lev), out_shape=jax.Sha...]
    reshape x13 -> x0, local copies, waits for them, and re-layouts: 31.7 us -> none  [the longest x10 22.8 us: block_apply(): blocks.astype(jnp.float32)]
    unnamed x57 -> x11, local copies, waits for them, and re-layouts: 1.84 us -> 18.8 us
    slice x3 -> x0, local copies, waits for them, and re-layouts: 13.1 us -> none  [the longest x1 8.49 us: finish_solve(): diag_inverse[:, block_id]]
    gather x2 -> x0, local copies, waits for them, and re-layouts: 5.6 us -> none  [the longest x1 2.83 us: per_device(): from_left = jnp.take(padded, neighbours[:, 0] - base_row, axis=0)]
    ppermute x2 -> x0, starting transfers between devices: 5.13 us -> none  [the longest x1 3.85 us: padded_2(): before = lax.ppermute(last, axis, up)]
  transfers between devices with their start and end apart: 2 -> 0, of which waited for: 0 -> 0; matrix products, arithmetic and copies ran while one was open for 28% -> 0% of each run, Pallas kernels for 0% -> 0%
where the time goes in v1:
time: 60.6 us; the launch traced here: 60.2 us
  Pallas kernels  41.4 us (68%)
  local copies, waits for them, and re-layouts  18.8 us (31%)
    pallas_call x1, Pallas kernels, per_device(): pl.pallas_call(functools.partial(kernel, n_dom, n_lev), out_shape=jax.Sha...  41.4 us
    unnamed x11, local copies, waits for them, and re-layouts  18.8 us

profile of v1, /device:TPU:0, one launch (start us, length us, event | category | flops | bytes accessed | tf_op | source)
XLA Modules:
  0.0 60.2 jit_solution(3857595134357438469)
XLA Ops:
  0.0 1.4 %copy.16.neigh = s32[32,2]{1,0:T(8,128)} copy(s32[32,2]{0,1:T(2,128)} %param.16) | data formatting | bytes 512 | tf_op args[1]
  1.4 1.4 %copy.17.pattern = s32[32,6]{1,0:T(8,128)} copy(s32[32,6]{0,1:T(8,128)} %param.17) | data formatting | bytes 1536 | tf_op args[2]
  2.7 1.7 %copy.22.l4i_h = bf16[384,192]{1,0:T(8,128)(2,1)} copy(bf16[384,192]{0,1:T(8,128)(2,1)} %param.27) | data formatting | bytes 294912 | tf_op args[12]
  4.5 1.8 %copy.23.l4r_h = bf16[384,192]{1,0:T(8,128)(2,1)} copy(bf16[384,192]{0,1:T(8,128)(2,1)} %param.28) | data formatting | bytes 294912 | tf_op args[13]
  6.2 0.0 copy-start
  6.2 2.0 %copy.20.l2i_h = bf16[768,192]{1,0:T(8,128)(2,1)} copy(bf16[768,192]{0,1:T(8,128)(2,1)} %param.23) | data formatting | bytes 589824 | tf_op args[8]
  8.2 1.9 %copy.21.l2r_h = bf16[768,192]{1,0:T(8,128)(2,1)} copy(bf16[768,192]{0,1:T(8,128)(2,1)} %param.24) | data formatting | bytes 589824 | tf_op args[9]
  10.1 3.7 %copy.18.lower_h = bf16[32,6,4096]{2,1,0:T(8,128)(2,1)} copy(bf16[32,6,4096]{2,0,1:T(8,128)(2,1)} %param.19) | data formatting | bytes 3145728 | tf_op args[4]
  13.8 0.0 copy-done
  13.8 2.8 %copy.19.l1_h = bf16[6144,192]{1,0:T(8,128)(2,1)} copy(bf16[6144,192]{0,1:T(8,128)(2,1)S(1)} %copy-done) | data formatting | bytes 4718592 | tf_op args[7]
  16.5 41.4 %shard_map.145 = f32[32,32,256]{2,1,0:T(8,128)} custom-call(s32[32,2]{1,0:T(8,128)} %copy.16.neigh, s32[32,6]{1,0:T(8,128)} %copy.17.pattern, s32[32]{0:T(128)} %agg.1, f32[32,32,256]{2,1,0:T(8,128)} %res_h.1, bf16[32,4,4096]{2,1,0:T(4,128)(2,1)} %diag_h.1, bf16[32,6,4096]{2,1,0:T(8,128)(2,1)} %copy.18.lower_h, bf16[32,192,256]{2,1,0:T(8,128)(2,1)} %phi_h.1, ...), custom_call_target="tpu_custom_call" | custom-call | flops 1000000000 | bytes 13000000 | tf_op jit(solution)/shard_map/pallas_call | solution.py:471
  57.9 2.3 %copy.25 = f32[32,32,256]{2,1,0:T(8,128)} copy(f32[32,32,256]{2,1,0:T(8,128)} %shard_map.145) | data formatting | bytes 2097152
Async XLA Ops:
  6.2 7.6 %copy-start = (bf16[6144,192]{0,1:T(8,128)(2,1)S(1)}, bf16[6144,192]{0,1:T(8,128)(2,1)}, u32[]{:S(2)}) copy-start(bf16[6144,192]{0,1:T(8,128)(2,1)} %param.22) | copy-start | bytes 7077892

commit v2 on v1

--- a/solution.py
+++ b/solution.py
@@ -11,7 +11,8 @@
 F32 = jnp.float32
 BF16 = jnp.bfloat16
 GROUP = 8
-UNROLL = 4
+UNROLL = 8
+CHUNK = 16
 
 
 def split(x):
@@ -31,6 +32,26 @@
 
 def mul_t(x, w):
     return fold(lax.dot_general(split(x), w, (((1,), (1,)), ((), ())), preferred_element_type=F32))
+
+
+def window(size, index):
+    low = index * size // 128 * 128
+    return low, -(-((index + 1) * size) // 128) * 128, index * size - low
+
+
+def mul_part(x, wt, off):
+    pad = []
+    if off:
+        pad.append(jnp.zeros((x.shape[0], off), F32))
+    pad.append(x)
+    rest = wt.shape[1] - off - x.shape[1]
+    if rest:
+        pad.append(jnp.zeros((x.shape[0], rest), F32))
+    return mul_t(jnp.concatenate(pad, axis=1) if len(pad) > 1 else x, wt)
+
+
+def mul_part_t(x, wt, off, size):
+    return mul(x, wt)[:, off : off + size]
 
 
 def near(ref, i):
@@ -71,6 +92,7 @@
     recv_l,
     recv_r,
     spread,
+    spread_d,
     wide,
     lmat,
     dmat,
@@ -91,7 +113,7 @@
     out_sem,
 ):
     subs, rhs, dofs = res.shape
-    npair = lower.shape[1]
+    npair = lower.shape[0]
     nblk = diag.shape[1]
     bs = dofs // nblk
     edge = 2 * bs
@@ -213,39 +235,46 @@
         b_odd = zero if b is None else b
         return jnp.where(low_lane, a_even, b_even), jnp.where(low_lane, a_odd, b_odd)
 
-    def unpack(s, carry):
-        x = lower[s].astype(F32)
-        y = diag[s].astype(F32)
-        for t in range(tiles):
-            spread[0, pl.ds(t * 8, npair), :] = x[:, t * 128 : (t + 1) * 128]
-            spread[1, pl.ds(t * 8, nblk), :] = y[:, t * 128 : (t + 1) * 128]
-
-        def block(kind, i):
-            return spread[kind, pl.ds(i, tiles, stride=8), :]
-
-        for b in range(nblk):
+    def unpack_chunk(c, carry):
+        first = pl.multiple_of(c * CHUNK, CHUNK)
+        for p in range(npair):
+            x = lower[p, pl.ds(first, CHUNK), :].astype(F32)
+            for t in range(tiles):
+                spread[p, pl.ds(t * CHUNK, CHUNK), :] = x[:, t * 128 : (t + 1) * 128]
+        lax.fori_loop(0, CHUNK // 2, functools.partial(unpack, c * CHUNK), 0)
+        return carry
+
+    def unpack(first, i, carry):
+        for u in range(2):
+            k = i * 2 + u
+            s = first + k
+            y = diag[s].astype(F32)
+            for t in range(tiles):
+                spread_d[u, pl.ds(t * 8, nblk), :] = y[:, t * 128 : (t + 1) * 128]
+            for b in range(nblk):
+                for jp in range(nblk // 2):
+                    if 2 * jp < b:
+                        parts = []
+                        for j in (2 * jp, 2 * jp + 1):
+                            if j < b:
+                                slot = b * (b - 1) // 2 + j
+                                rows = spread[slot, pl.ds(k, tiles, stride=CHUNK), :]
+                                parts.append(rows * pattern[slot, s].astype(F32))
+                            else:
+                                parts.append(None)
+                        even, odd = pair_rows(*parts)
+                        wide[u, jp, pl.ds(b * bs, tiles, stride=2), :] = even
+                        wide[u, jp, pl.ds(b * bs + 1, tiles, stride=2), :] = odd
+                own = spread_d[u, pl.ds(b, tiles, stride=8), :]
+                even, odd = pair_rows(*((own, None) if b % 2 == 0 else (None, own)))
+                wide[u, nblk // 2, pl.ds(b * bs, tiles, stride=2), :] = even
+                wide[u, nblk // 2, pl.ds(b * bs + 1, tiles, stride=2), :] = odd
             for jp in range(nblk // 2):
-                if 2 * jp < b:
-                    parts = []
-                    for j in (2 * jp, 2 * jp + 1):
-                        if j < b:
-                            slot = b * (b - 1) // 2 + j
-                            parts.append(block(0, slot) * pattern[s, slot].astype(F32))
-                        else:
-                            parts.append(None)
-                    even, odd = pair_rows(*parts)
-                    wide[jp, pl.ds(b * bs, tiles, stride=2), :] = even
-                    wide[jp, pl.ds(b * bs + 1, tiles, stride=2), :] = odd
-            own = block(1, b)
-            even, odd = pair_rows(*((own, None) if b % 2 == 0 else (None, own)))
-            wide[nblk // 2, pl.ds(b * bs, tiles, stride=2), :] = even
-            wide[nblk // 2, pl.ds(b * bs + 1, tiles, stride=2), :] = odd
-        for jp in range(nblk // 2):
-            lmat[s, :, pl.ds(jp * 128, 128)] = wide[jp].astype(BF16)
-        dmat[s] = wide[nblk // 2].astype(BF16)
+                lmat[s, :, pl.ds(jp * 128, 128)] = wide[u, jp].astype(BF16)
+            dmat[s] = wide[u, nblk // 2].astype(BF16)
         return carry
 
-    lax.fori_loop(0, subs, unpack, 0)
+    lax.fori_loop(0, subs // CHUNK, unpack_chunk, 0)
 
     for copy in loads[2:5]:
         copy.wait()
@@ -271,21 +300,27 @@
     base_l = jnp.maximum(me - 1, 0) * subs
     base_r = jnp.minimum(me + 1, last) * subs
     agg_base = me * n_agg
+
+    def l1_part(g, u):
+        low, high, off = window(width, u)
+        first = pl.multiple_of(g * (UNROLL * width) + low, 128)
+        return l1[:, pl.ds(first, high - low)], off
+
+    def part_of(ref, a):
+        low, high, off = window(width, a)
+        return ref[:, pl.ds(low, high - low)], off
 
     def up(g, carry):
         ids = [g * UNROLL + u for u in range(UNROLL)]
         full = []
         for s in ids:
             mine = res[s]
-            total = mine[:, inner:] + near(recv_l, neigh[s, 0] - base_l) + near(recv_r, neigh[s, 1] - base_r)
+            total = mine[:, inner:] + near(recv_l, neigh[0, s] - base_l) + near(recv_r, neigh[1, s] - base_r)
             full.append(jnp.concatenate([mine[:, :inner], total / 3.0], axis=1))
         for s, x in zip(ids, full):
             res[s] = x
         coarse = [mul_t(x, phi[s]) for s, x in zip(ids, full)]
-        terms = [
-            mul(x, l1[pl.ds(pl.multiple_of(s * width, width), width), :])
-            for s, x in zip(ids, coarse)
-        ]
+        terms = [mul_part(x, *l1_part(g, u)) for u, x in enumerate(coarse)]
         for a in range(n_agg):
             acc = l2res[a]
             for s, x in zip(ids, terms):
@@ -337,9 +372,9 @@
     def work(i):
         lax.fori_loop(cuts[i], cuts[i + 1], fine_step, 0)
 
-    part = mul(l2res[0], l2r[pl.ds(0, width), :])
+    part = mul_part(l2res[0], *part_of(l2r, 0))
     for a in range(1, n_agg):
-        part = part + mul(l2res[a], l2r[pl.ds(a * width, width), :])
+        part = part + mul_part(l2res[a], *part_of(l2r, a))
     copy = exchange(0, part)
     work(0)
     copy.wait()
@@ -368,23 +403,23 @@
     for copy in sends:
         copy.wait()
 
-    top_res = mul(totals[0], l4r[pl.ds(0, width), :])
+    top_res = mul_part(totals[0], *part_of(l4r, 0))
     for p in range(1, n_groups):
-        top_res = top_res + mul(totals[p], l4r[pl.ds(p * width, width), :])
+        top_res = top_res + mul_part(totals[p], *part_of(l4r, p))
     top_corr = mul_t(top_res, top[...])
-    at_group = pl.ds(pl.multiple_of(group * width, width), width)
-    l4corr = mul_t(totals[group], l4i[at_group, :]) + mul_t(top_corr, l4r[at_group, :])
+    two = pl.ds(pl.multiple_of(group // 2 * (2 * width), 128), 2 * width)
+    l4two = mul(totals[group], l4i[:, two]) + mul(top_corr, l4r[:, two])
+    l4corr = jnp.where(group % 2 == 0, l4two[:, :width], l4two[:, width:])
     l3corr = mul_t(xsend[0] + xrecv[0], l3i[...]) + mul_t(l4corr, l3r[...])
     for a in range(n_agg):
-        rows = pl.ds(a * width, width)
-        l2corr[a] = mul_t(l2res[a], l2i[rows, :]) + mul_t(l3corr, l2r[rows, :])
+        l2corr[a] = mul_part_t(l2res[a], *part_of(l2i, a), width) + mul_part_t(
+            l3corr, *part_of(l2r, a), width
+        )
 
     def down(g, carry):
         ids = [g * UNROLL + u for u in range(UNROLL)]
         q = [near(l2corr, agg[s] - agg_base) for s in ids]
-        coarse = [
-            mul_t(x, l1[pl.ds(pl.multiple_of(s * width, width), width), :]) for s, x in zip(ids, q)
-        ]
+        coarse = [mul_part_t(x, *l1_part(g, u), width) for u, x in enumerate(q)]
         both = [mul(x, phi[s]) for s, x in zip(ids, coarse)]
         for s, x in zip(ids, both):
             fine[s] = fine[s] + x
@@ -430,26 +465,28 @@
         n_agg = subs // 8
         n_groups = n_dom // GROUP
         n_x = 4
+        lower_t = lower_blocks.transpose(1, 0, 2)
         large = [
             residual,
             diag_inverse,
-            lower_blocks,
+            lower_t,
             phi,
-            level1_restrict,
-            level2_interior_solve,
-            level2_restrict,
+            level1_restrict.T,
+            level2_interior_solve.T,
+            level2_restrict.T,
             level3_interior_solve,
             level3_restrict,
-            level4_interior_solve,
-            level4_restrict,
+            level4_interior_solve.T,
+            level4_restrict.T,
             top_inverse,
         ]
         scratch = [pltpu.VMEM(a.shape, a.dtype) for a in large]
         scratch += [
             pltpu.VMEM((subs, rhs, edge), F32),
             pltpu.VMEM((subs, rhs, edge), F32),
+            pltpu.VMEM((lower_t.shape[0], tiles * CHUNK, 128), F32),
             pltpu.VMEM((2, tiles * 8, 128), F32),
-            pltpu.VMEM((nblk // 2 + 1, dofs, 128), F32),
+            pltpu.VMEM((2, nblk // 2 + 1, dofs, 128), F32),
             pltpu.VMEM((subs, dofs, dofs), BF16),
             pltpu.VMEM((subs, dofs, 128), BF16),
             pltpu.VMEM((subs, rhs, dofs), F32),
@@ -481,7 +518,7 @@
             cost_estimate=pl.CostEstimate(
                 flops=10**9, bytes_accessed=13 * 10**6, transcendentals=0
             ),
-        )(neighbours, pattern, aggregate, *large)
+        )(neighbours.T, pattern.T, aggregate, *large)
 
     both = P(("dom", "level"))
     in_specs = (both,) * 10 + (P("dom"),) * 2 + (P(),) * 3

time: 60.6 us -> 41.5 us (0.68)
  local copies, waits for them, and re-layouts: 18.8 us -> 2.31 us
  Pallas kernels: 41.4 us -> 39 us
    unnamed x11 -> x1, local copies, waits for them, and re-layouts: 18.8 us -> 2.31 us
    pallas_call x1, Pallas kernels: 41.4 us -> 39 us  [per_device(): pl.pallas_call(functools.partial(kernel, n_dom, n_lev), out_shape=jax.Sha...]
where the time goes in v2:
time: 41.5 us; the launch traced here: 41.4 us
  Pallas kernels  39 us (94%)
  local copies, waits for them, and re-layouts  2.31 us (6%)
    pallas_call x1, Pallas kernels, per_device(): pl.pallas_call(functools.partial(kernel, n_dom, n_lev), out_shape=jax.Sha...  39 us
    unnamed x1, local copies, waits for them, and re-layouts  2.31 us

profile of v2, /device:TPU:0, one launch (start us, length us, event | category | flops | bytes accessed | tf_op | source)
XLA Modules:
  0.0 41.4 jit_solution(9625656284443656220)
XLA Ops:
  0.0 39.0 %shard_map.145 = f32[32,32,256]{2,1,0:T(8,128)} custom-call(s32[2,32]{1,0:T(2,128)} %bitcast.15, s32[6,32]{1,0:T(8,128)} %bitcast.14, s32[32]{0:T(128)} %agg.1, f32[32,32,256]{2,1,0:T(8,128)} %res_h.1, bf16[32,4,4096]{2,1,0:T(4,128)(2,1)} %diag_h.1, bf16[6,32,4096]{2,1,0:T(8,128)(2,1)} %bitcast.9, bf16[32,192,256]{2,1,0:T(8,128)(2,1)} %phi_h.1, ...), custom_call_target="tpu_custom_call" | custom-call | flops 1000000000 | bytes 13000000 | tf_op jit(solution)/shard_map/pallas_call | solution.py:508
  39.0 2.3 %copy.17 = f32[32,32,256]{2,1,0:T(8,128)} copy(f32[32,32,256]{2,1,0:T(8,128)} %shard_map.145) | data formatting | bytes 2097152
